TPU v7x, 256 devices: a whole 4x4x8 slice. The times are simulated.
256 devices in a mesh: pipe: 2 (over x_hi), ctx: 32 (over y, z), dp: 4 (over x_lo, core).
Axes of the slice: x: 4 (x_hi: 2, x_lo: 2; x = x_hi * 2 + x_lo), y: 4, z: 8, core: 2. Of those that a mesh axis runs over, the one named last changes fastest.
Arguments:
- queries: bfloat16 [4, 16384, 2048], P('dp', 'ctx', 'pipe'), may hold values from -8 to 8
- keys: bfloat16 [4, 16384, 2048], P('dp', 'ctx', 'pipe'), may hold values from -8 to 8
- values: bfloat16 [4, 16384, 2048], P('dp', 'ctx', 'pipe'), may hold values from -6 to 6
- outputs: bfloat16 [4, 16384, 2048], P('dp', 'ctx', 'pipe'), may hold values from -6 to 6
- out_grads: bfloat16 [4, 16384, 2048], P('dp', 'ctx', 'pipe'), may hold values from -6 to 6
- lengths: int32 [4, 4], P('dp'), may hold values from 1 to 8192, 16384 in all within a row
- proj_weight: bfloat16 [3, 512, 2048], P(None, None, 'pipe'), may hold values from -1.5 to 1.5
- hidden: bfloat16 [4, 32768, 512], P('dp', 'ctx'), may hold values from -0.078125 to 0.078125
- conv_weight: bfloat16 [4, 512, 512], P(None, None, 'pipe'), may hold values from -0.125 to 0.125
Outputs:
- hidden_grad: bfloat16 [4, 32768, 512], P('dp', 'ctx', 'pipe')
- conv_grad: float32 [4, 512, 512], P(None, 'ctx', 'pipe')
Inputs may be any that keep to these rules, and one draw needn't show every extreme that they name: Each sequence has 1 to 8192 latent frames, the 4 lengths of a group add up to 16384, and the longest is exactly 8192.
All inputs are finite; a program needn't handle non-finite values.
Results may differ from a plain program's by a relative error of at most 0.0063.
Values may be sent and summed in bfloat16 or wider, within the bound.
A program may use at most 128 MiB of HBM per device.

v0:
```python
import jax
import jax.numpy as jnp
from jax import lax
from jax.sharding import PartitionSpec as P

HEAD_DIM = 128


masked_score = -1e30
tap_offsets = (-2, -1, -1, 0)


def from_behind(shard, axis, by):
    size = lax.axis_size(axis)
    pairs = [(i, i + by) for i in range(size) if 0 <= i + by < size]
    return lax.ppermute(shard, axis, pairs)


def segment_of(ends, positions):
    counted = jnp.sum((ends[None, :] <= positions[:, None]).astype(jnp.int32), axis=1)
    return jnp.where(positions >= 0, counted, -1)


def block_mask(ends, query_start, key_start, count, frames):
    offsets = jnp.arange(count, dtype=jnp.int32)
    query_pos = query_start + offsets
    key_pos = key_start + offsets
    query_seg = jnp.where(query_pos < frames, segment_of(ends, query_pos), -2)
    key_seg = segment_of(ends, key_pos)
    allowed = (query_seg[:, None] == key_seg[None, :]) & (key_pos[None, :] <= query_pos[:, None])
    return (allowed, jnp.any(allowed))


def softmax_stats(query_heads, key_heads, allowed, running, scale):
    running_max, running_sum = running
    scores = (
        jnp.einsum("qhd,khd->hqk", query_heads, key_heads, preferred_element_type=jnp.float32)
        * scale
    )
    block_max = jnp.max(jnp.where(allowed[None], scores, masked_score), axis=-1)
    new_max = jnp.maximum(running_max, block_max)
    weights = jnp.where(allowed[None], jnp.exp(scores - new_max[..., None]), 0.0)
    return (new_max, running_sum * jnp.exp(running_max - new_max) + jnp.sum(weights, axis=-1))


def pair_grads(query_heads, grad_heads, log_total, delta, key_heads, value_heads, allowed, scale):
    scores = (
        jnp.einsum("qhd,khd->hqk", query_heads, key_heads, preferred_element_type=jnp.float32)
        * scale
    )
    prob = jnp.where(allowed[None], jnp.exp(scores - log_total[..., None]), 0.0)
    dprob = jnp.einsum("qhd,khd->hqk", grad_heads, value_heads, preferred_element_type=jnp.float32)
    dscore = (prob * (dprob - delta[..., None])).astype(jnp.bfloat16)
    prob_low = prob.astype(jnp.bfloat16)
    value_grad = jnp.einsum(
        "hqk,qhd->khd", prob_low, grad_heads, preferred_element_type=jnp.float32
    )
    key_grad = (
        jnp.einsum("hqk,qhd->khd", dscore, query_heads, preferred_element_type=jnp.float32) * scale
    )
    query_grad = (
        jnp.einsum("hqk,khd->qhd", dscore, key_heads, preferred_element_type=jnp.float32) * scale
    )
    return (query_grad, key_grad, value_grad)


def guarded_grads(
    query_heads, grad_heads, log_total, delta, key_heads, value_heads, allowed, scale
):

    def compute():
        return pair_grads(
            query_heads, grad_heads, log_total, delta, key_heads, value_heads, allowed, scale
        )

    return compute()


def guarded_stats(query_heads, key_heads, allowed, running, scale):

    def compute():
        return softmax_stats(query_heads, key_heads, allowed, running, scale)

    return compute()


def transposed(left, right):
    return lax.dot_general(
        left, right, (((1,), (1,)), ((), ())), preferred_element_type=jnp.float32
    )


def body(queries, keys, values, outputs, out_grads, lengths, proj_weight, hidden, conv_weight):
    rows = queries.shape[1]
    local_width = queries.shape[2]
    local_heads = local_width // HEAD_DIM
    scale = HEAD_DIM ** (-0.5)
    cycle_index = lax.axis_index("ctx")
    cycle_size = lax.axis_size("ctx")
    frames = rows * cycle_size
    my_start = cycle_index * rows
    ends = jnp.cumsum(lengths[0])

    def to_heads(block):
        return block.reshape(rows, local_heads, HEAD_DIM)

    def flat(block):
        return block.reshape(rows, local_width)

    query_heads = to_heads(queries[0])
    grad_heads = to_heads(out_grads[0])
    output_heads = to_heads(outputs[0])
    key_heads = to_heads(keys[0])
    value_heads = to_heads(values[0])
    delta = jnp.einsum("qhd,qhd->hq", grad_heads, output_heads, preferred_element_type=jnp.float32)
    own_mask, own_active = block_mask(ends, my_start, my_start, rows, frames)
    running = (
        jnp.full((local_heads, rows), masked_score, jnp.float32),
        jnp.zeros((local_heads, rows), jnp.float32),
    )
    running = guarded_stats(query_heads, key_heads, own_mask, running, scale)
    key_pair = (keys[0], values[0])
    distance = 1
    key_pair = from_behind((key_pair[0], key_pair[1]), "ctx", 1)
    allowed, active = block_mask(ends, my_start, (cycle_index - distance) * rows, rows, frames)
    running = guarded_stats(query_heads, to_heads(key_pair[0]), allowed, running, scale)
    remote = [(key_pair, allowed, active)]
    log_total = running[0] + jnp.log(running[1])
    query_part, key_part, value_part = guarded_grads(
        query_heads, grad_heads, log_total, delta, key_heads, value_heads, own_mask, scale
    )
    query_acc = flat(query_part)
    key_acc = flat(key_part)
    value_acc = flat(value_part)
    distance = 1
    pair, allowed, active = remote[distance - 1]
    query_part, key_part, value_part = guarded_grads(
        query_heads,
        grad_heads,
        log_total,
        delta,
        to_heads(pair[0]),
        to_heads(pair[1]),
        allowed,
        scale,
    )
    query_acc = query_acc + flat(query_part)
    returned = from_behind((flat(key_part), flat(value_part)), "ctx", -distance)
    key_acc = key_acc + returned[0]
    value_acc = value_acc + returned[1]
    latent_part = transposed(query_acc.astype(jnp.bfloat16), proj_weight[0])
    latent_part = latent_part + transposed(key_acc.astype(jnp.bfloat16), proj_weight[1])
    latent_part = latent_part + transposed(value_acc.astype(jnp.bfloat16), proj_weight[2])
    latent = lax.psum_scatter(latent_part, "pipe", scatter_dimension=1, tiled=True).astype(
        jnp.bfloat16
    )
    features = hidden[0]
    paired = features.reshape(rows, 2, features.shape[1])
    tail = from_behind(features[2 * rows - 4 :], "ctx", 1)
    ext_even = jnp.concatenate([tail[0:4:2], paired[:, 0]], axis=0)
    ext_odd = jnp.concatenate([tail[1:4:2], paired[:, 1]], axis=0)
    tap_rows = (
        ext_odd[0:rows],
        ext_even[1 : rows + 1],
        ext_odd[1 : rows + 1],
        ext_even[2 : rows + 2],
    )
    frame_pos = my_start + jnp.arange(rows, dtype=jnp.int32)
    frame_seg = segment_of(ends, frame_pos)
    tap_list = []
    for tap in range(4):
        tap_live = segment_of(ends, frame_pos + tap_offsets[tap]) == frame_seg
        masked_rows = jnp.where(tap_live[:, None], tap_rows[tap], jnp.zeros_like(tap_rows[tap]))
        tap_list.append(
            lax.dot_general(
                masked_rows, latent, (((0,), (0,)), ((), ())), preferred_element_type=jnp.float32
            )
        )
    local_taps = jnp.stack(tap_list, axis=0)
    head = from_behind(latent[0:2], "ctx", -1)
    ext_latent = jnp.concatenate([latent, head], axis=0)
    ext_pos = my_start + jnp.arange(rows + 2, dtype=jnp.int32)
    ext_seg = segment_of(ends, ext_pos)
    masked_latent = []
    for tap in range(4):
        tap_live = segment_of(ends, ext_pos + tap_offsets[tap]) == ext_seg
        masked_latent.append(jnp.where(tap_live[:, None], ext_latent, jnp.zeros_like(ext_latent)))
    even_grad = transposed(masked_latent[3][0:rows], conv_weight[3]) + transposed(
        masked_latent[1][1 : rows + 1], conv_weight[1]
    )
    odd_grad = transposed(masked_latent[2][1 : rows + 1], conv_weight[2]) + transposed(
        masked_latent[0][2 : rows + 2], conv_weight[0]
    )
    hidden_part = jnp.stack([even_grad, odd_grad], axis=1).reshape(2 * rows, even_grad.shape[1])
    hidden_grad = lax.psum_scatter(hidden_part, "pipe", scatter_dimension=1, tiled=True).astype(
        jnp.bfloat16
    )
    total = lax.psum(local_taps, ("ctx", "dp"))
    share = total.shape[1] // cycle_size
    conv_grad = lax.dynamic_slice_in_dim(total, cycle_index * share, share, 1)
    return (hidden_grad[None], conv_grad)


def solution(mesh):
    placed = (
        P("dp", "ctx", "pipe"),
        P("dp", "ctx", "pipe"),
        P("dp", "ctx", "pipe"),
        P("dp", "ctx", "pipe"),
        P("dp", "ctx", "pipe"),
        P("dp", None),
        P(None, None, "pipe"),
        P("dp", "ctx", None),
        P(None, None, "pipe"),
    )
    return jax.shard_map(
        body,
        mesh=mesh,
        in_specs=placed,
        out_specs=(P("dp", "ctx", "pipe"), P(None, "ctx", "pipe")),
        check_vma=False,
    )
```

profile of v0, /device:TPU:1, one launch (start us, length us, event | category | flops | bytes accessed | tf_op | source)
XLA Modules:
  0.0 1314.7 jit_solution(207221607958176256)
XLA Ops:
  7.2 1.6 copy.154
  8.8 5.4 collective-permute-start
  14.2 2.3 copy.118
  16.5 3.6 collective-permute-start.1
  20.7 1.6 copy.158
  22.2 0.6 fusion.16
  22.9 1.5 copy.128
  24.4 1.5 copy.155
  26.0 1.3 copy.156
  27.3 0.6 compare_and_fusion.1
  27.9 1.6 select_reduce_fusion.3
  29.5 5.5 collective-permute-done
  35.0 2.9 select_reduce_fusion.2
  37.9 1.7 select_reduce_fusion.1
  39.6 1.7 select_reduce_fusion
  41.4 3.2 fusion.2
  44.6 1.5 collective-permute-start.3
  46.1 11.5 collective-permute-done.1
  57.6 4.3 multiply_convert_fusion
  61.9 1.5 convolution_multiply_fusion
  63.4 1.3 collective-permute-start.2
  64.8 2.8 multiply_convert_fusion.1
  67.6 0.7 fusion.85
  68.3 2.0 multiply_convert_fusion.2
  70.3 2.0 fusion.21
  72.3 1.5 convolution_multiply_fusion.1
  73.8 1.9 fusion.4
  75.7 61.7 %collective-permute-done.2 = f32[512,1024]{0,1:T(8,128)} collective-permute-done((f32[512,1024]{0,1:T(8,128)S(1)}, f32[512,1024]{0,1:T(8,128)}, u32[]{:S(2)}, u32[]{:S(2)}) %collective-permute-start.2) | collective-permute-done | bytes 2097184 | tf_op jit(solution)/shard_map/ppermute | solution.py:16
  137.3 2.0 fusion.15
  139.4 0.8 convolution_add_fusion.1
  140.2 2.1 fusion.14
  142.3 1.7 convolution_add_fusion
  144.2 3.7 collective-permute-start.5
  148.3 1.5 fusion.84
  150.2 27.6 %reduce-scatter.3.cloned.1.call-done = f32[512,256]{1,0:T(8,128)} async-done(((f32[512,512]{1,0:T(8,128)}), f32[512,256]{1,0:T(8,128)}) %reduce-scatter.3.cloned.1.call-update) | async-done | bytes 524304 | tf_op jit(solution)/shard_map/reduce_scatter | solution.py:154
  177.8 1.1 convert_element_type.72
  179.2 0.5 convolution_bitcast_fusion.2
  179.7 0.5 convolution_bitcast_fusion.1
  180.2 0.5 convolution_bitcast_fusion.3
  180.7 1.5 pad_maximum_fusion.1
  182.5 1.3 collective-permute-start.4
  184.1 2.7 collective-permute-done.4
  188.1 1.6 copy.131
  189.7 2.5 reshape.289
  192.2 1074.9 %all-reduce.2.cloned.1.call-done = f32[4,512,256]{2,1,0:T(8,128)} async-done(((f32[4,512,256]{2,1,0:T(8,128)}), f32[4,512,256]{2,1,0:T(8,128)}) %all-reduce.2.cloned.1.call-update) | async-done | bytes 2097168 | tf_op jit(solution)/shard_map/psum | solution.py:198
  1267.0 1.5 constant_dynamic-slice_fusion
  1268.5 37.6 %reduce-scatter.5.cloned.1.call-done = f32[1024,256]{1,0:T(8,128)} async-done(((f32[1024,512]{1,0:T(8,128)}), f32[1024,256]{1,0:T(8,128)}) %reduce-scatter.5.cloned.1.call-update) | async-done | bytes 1048592 | tf_op jit(solution)/shard_map/reduce_scatter | solution.py:195
  1306.1 2.1 convert_bitcast_fusion
  (53 shorter events, 3.9 us)
Async XLA Ops:
  7.2 12.9 copy-start.7
  7.2 13.2 %copy-start.3 = (bf16[1,512,1024]{2,1,0:T(8,128)(2,1)S(1)}, bf16[1,512,1024]{2,1,0:T(8,128)(2,1)}, u32[]{:S(2)}) copy-start(bf16[1,512,1024]{2,1,0:T(8,128)(2,1)} %param.13) | copy-start | bytes 3145732
  7.2 170.6 %reduce-scatter.3.cloned.1.call-start = ((), (), s32[]{:S(2)}) async-start(), calls=%async_computation.2 | async-start | bytes 1572864 | tf_op jit(solution)/shard_map/reduce_scatter | solution.py:154
  8.8 26.2 %collective-permute-start = (bf16[512,1024]{0,1:T(8,128)(2,1)S(1)}, bf16[512,1024]{0,1:T(8,128)(2,1)}, u32[]{:S(2)}, u32[]{:S(2)}) collective-permute-start(bf16[512,1024]{0,1:T(8,128)(2,1)S(1)} %bitcast.117), channel_id=1, source_target_pairs={{0,4},{4,8},{8,12},{12,16},{16,20},{20,24},{24,28},{28,32},{32,36}... | collective-permute-start | bytes 3145736 | tf_op jit(solution)/shard_map/ppermute | solution.py:16
  16.5 41.1 %collective-permute-start.1 = (bf16[512,1024]{0,1:T(8,128)(2,1)}, bf16[512,1024]{0,1:T(8,128)(2,1)}, u32[]{:S(2)}, u32[]{:S(2)}) collective-permute-start(bf16[512,1024]{0,1:T(8,128)(2,1)} %bitcast.6), channel_id=1, source_target_pairs={{0,4},{4,8},{8,12},{12,16},{16,20},{20,24},{24,28},{28,32},{32,36}... | collective-permute-start | bytes 3145736 | tf_op jit(solution)/shard_map/ppermute | solution.py:16
  20.6 5.4 copy-start
  39.6 1.8 copy-start.4
  44.6 95.5 %collective-permute-start.3 = (f32[512,1024]{0,1:T(8,128)}, f32[512,1024]{0,1:T(8,128)}, u32[]{:S(2)}, u32[]{:S(2)}) collective-permute-start(f32[512,1024]{0,1:T(8,128)} %bitcast.19), channel_id=1, source_target_pairs={{4,0},{8,4},{12,8},{16,12},{20,16},{24,20},{28,24},{32,28},{36,32}... | collective-permute-start | bytes 6291464 | tf_op jit(solution)/shard_map/ppermute | solution.py:16
  61.9 2.8 copy-start.5
  63.4 73.9 %collective-permute-start.2 = (f32[512,1024]{0,1:T(8,128)S(1)}, f32[512,1024]{0,1:T(8,128)}, u32[]{:S(2)}, u32[]{:S(2)}) collective-permute-start(f32[512,1024]{0,1:T(8,128)S(1)} %bitcast.122), channel_id=1, source_target_pairs={{4,0},{8,4},{12,8},{16,12},{20,16},{24,20},{28,24},{32,28},{36,32}... | collective-permute-start | bytes 6291464 | tf_op jit(solution)/shard_map/ppermute | solution.py:16
  75.6 63.7 %copy-start.1 = (bf16[3,512,1024]{2,1,0:T(8,128)(2,1)S(1)}, bf16[3,512,1024]{2,1,0:T(8,128)(2,1)}, u32[]{:S(2)}) copy-start(bf16[3,512,1024]{2,1,0:T(8,128)(2,1)} %param.15) | copy-start | bytes 9437188
  140.2 4.0 copy-start.2
  144.1 1123.0 %all-reduce.2.cloned.1.call-start = ((), (), s32[]{:S(2)}) async-start(), calls=%async_computation.4 | async-start | bytes 4194304 | tf_op jit(solution)/shard_map/psum | solution.py:198
  144.2 5.9 collective-permute-start.5
  180.2 3.6 copy-start.6
  182.2 1123.9 %reduce-scatter.5.cloned.1.call-start = ((), (), s32[]{:S(2)}) async-start(), calls=%async_computation.3 | async-start | bytes 3145728 | tf_op jit(solution)/shard_map/reduce_scatter | solution.py:195
  182.5 4.3 collective-permute-start.4
Sparse Core Ops, SparseCore 0:
  144.2 33.5 reduce-scatter.2
  182.3 1084.7 all-reduce.1
  1269.6 36.5 reduce-scatter.4
where the time goes:
time: 1320 us; the launch traced here: 1310 us
  waiting for transfers between devices  1220 us (92%)
  matrix products  30.1 us (2%)
  local copies, waits for them, and re-layouts  18.1 us (1%)
  starting transfers between devices  16.8 us (1%)
  between operations  14.2 us (1%)
  other arithmetic  14.1 us (1%)
    psum x1, waiting for transfers between devices, body(): total = lax.psum(local_taps, ('ctx', 'dp'))  1070 us
    ppermute x6, waiting for transfers between devices, from_behind(): return lax.ppermute(shard, axis, pairs)  81.3 us
    reduce_scatter x1, waiting for transfers between devices, body(): lax.psum_scatter(hidden_part, 'pipe', scatter_dimension=1, tiled=True)  37.6 us
    reduce_scatter x1, waiting for transfers between devices, body(): lax.psum_scatter(latent_part, 'pipe', scatter_dimension=1, tiled=True)  27.6 us
  transfers between devices with their start and end apart: 9, of which 7 were waited for; matrix products, arithmetic and copies ran while one was open for 4% of the time, Pallas kernels for 0%

commit v1 on v0

v1 whole, which is shorter than its diff:
```python
import functools
import jax
import jax.numpy as jnp
from jax import lax
from jax.experimental import pallas as pl
from jax.experimental.pallas import tpu as pltpu
from jax.sharding import PartitionSpec as P

HEAD_DIM = 128
SCALE = HEAD_DIM ** (-0.5)
SCALE_LOG2E = SCALE * 1.4426950408889634
MASKED = -1e30
CHUNKS = 4
MESH = pl.DeviceIdType.MESH
F32 = jnp.float32
BF16 = jnp.bfloat16


def nn(left, right):
    return lax.dot_general(left, right, (((1,), (0,)), ((), ())), preferred_element_type=F32)


def nt(left, right):
    return lax.dot_general(left, right, (((1,), (1,)), ((), ())), preferred_element_type=F32)


def tn(left, right):
    return lax.dot_general(left, right, (((0,), (0,)), ((), ())), preferred_element_type=F32)


def kernel(
    n_ctx,
    lengths,
    q_in,
    k_in,
    v_in,
    o_in,
    g_in,
    w_in,
    hid_in,
    cw_in,
    hid_out,
    conv_out,
    q,
    k,
    v,
    o,
    g,
    w,
    hid,
    cw,
    k_prev,
    v_prev,
    q_next,
    g_next,
    bias_own,
    bias_prev,
    bias_next,
    e_own,
    e_next,
    stat_own,
    stat_next,
    stat_from_next,
    stat_from_prev,
    dq,
    dk,
    dv,
    dk_prev,
    dv_prev,
    dq_next,
    lat_sum,
    back_out,
    back_in,
    fwd_out,
    fwd_in,
    pipe_out,
    pipe_in,
    half_mine,
    half_other,
    ext,
    head_in,
    tail_in,
    taps_mine,
    taps_out,
    taps_in,
    spread,
    conv_part,
    conv_in,
    total,
    local_sem,
    kv_send,
    kv_recv,
    qg_send,
    qg_recv,
    stat_send,
    stat_recv,
    chunk_send,
    chunk_recv,
    misc_send,
    misc_recv,
    rs_send,
    rs_recv,
    dp_send,
    dp_recv,
):
    rows, width = q.shape
    heads = width // HEAD_DIM
    half_heads = heads // 2
    half_width = half_heads * HEAD_DIM
    ch = w.shape[1]
    half = ch // 2
    frames = rows * n_ctx
    share = ch // n_ctx
    chunk = rows // CHUNKS
    pipe = lax.axis_index("pipe")
    ctx = lax.axis_index("ctx")
    dp = lax.axis_index("dp")
    core = lax.rem(dp, 2)
    after = lax.rem(ctx + 1, n_ctx)
    before = lax.rem(ctx + n_ctx - 1, n_ctx)
    other_core = dp + 1 - 2 * core
    start = ctx * rows

    def cols(index):
        return pl.ds(pl.multiple_of(index * HEAD_DIM, HEAD_DIM), HEAD_DIM)

    def remote(src, dst, send, recv, where):
        return pltpu.make_async_remote_copy(
            src_ref=src,
            dst_ref=dst,
            send_sem=send,
            recv_sem=recv,
            device_id=where,
            device_id_type=MESH,
        )

    my_half = pl.ds(pl.multiple_of(pipe * half, half), half)
    their_half = pl.ds(pl.multiple_of((1 - pipe) * half, half), half)
    loads = [
        pltpu.make_async_copy(src, dst, local_sem.at[i])
        for i, (src, dst) in enumerate(
            (
                (hid_in, hid),
                (k_in, k),
                (q_in, q),
                (g_in, g),
                (o_in, o),
                (v_in, v),
                (w_in, w),
                (cw_in.at[:, my_half, :], cw.at[:, :, my_half]),
            )
        )
    ]
    for load in loads:
        load.start()

    barrier = pltpu.get_barrier_semaphore()

    def greet(step, carry):
        pl.semaphore_signal(
            barrier, inc=1, device_id={"ctx": lax.rem(ctx + step, n_ctx)}, device_id_type=MESH
        )
        return carry

    lax.fori_loop(1, n_ctx, greet, 0)
    pl.semaphore_signal(barrier, inc=1, device_id={"pipe": 1 - pipe}, device_id_type=MESH)
    for step in range(1, 4):
        pl.semaphore_signal(
            barrier, inc=1, device_id={"dp": lax.rem(dp + step, 4)}, device_id_type=MESH
        )
    pl.semaphore_wait(barrier, n_ctx - 1 + 1 + 3)

    tail = remote(
        hid_in.at[pl.ds(2 * rows - 16, 16), :],
        tail_in,
        misc_send.at[0],
        misc_recv.at[0],
        {"ctx": after},
    )
    tail.start()

    def kv_copies(index):
        return (
            remote(
                k_in.at[:, cols(index)],
                k_prev.at[:, cols(index)],
                kv_send.at[index, 0],
                kv_recv.at[index, 0],
                {"ctx": after},
            ),
            remote(
                v_in.at[:, cols(index)],
                v_prev.at[:, cols(index)],
                kv_send.at[index, 1],
                kv_recv.at[index, 1],
                {"ctx": after},
            ),
        )

    def qg_copies(index):
        return (
            remote(
                q_in.at[:, cols(half_heads + index)],
                q_next.at[:, cols(index)],
                qg_send.at[index, 0],
                qg_recv.at[index, 0],
                {"ctx": before},
            ),
            remote(
                g_in.at[:, cols(half_heads + index)],
                g_next.at[:, cols(index)],
                qg_send.at[index, 1],
                qg_recv.at[index, 1],
                {"ctx": before},
            ),
        )

    def halo(index, carry):
        for copy in qg_copies(index) + kv_copies(index):
            copy.start()
        return carry

    lax.fori_loop(0, half_heads, halo, 0)
    swap = remote(
        cw_in.at[:, their_half, :],
        cw.at[:, :, my_half],
        misc_send.at[1],
        misc_recv.at[1],
        {"pipe": 1 - pipe},
    )
    swap.start()

    ends = [lengths[0]]
    for i in range(1, 4):
        ends.append(ends[-1] + lengths[i])

    def segment(pos):
        count = jnp.zeros(pos.shape, jnp.int32)
        for end in ends:
            count = count + jnp.where(pos >= end, 1, 0)
        return jnp.where(pos >= 0, count, -1)

    row_pos = start + lax.broadcasted_iota(jnp.int32, (1, rows), 1)
    col_pos = start + lax.broadcasted_iota(jnp.int32, (rows, 1), 0)
    own_row = segment(row_pos)
    own_col = segment(col_pos)
    next_row = jnp.where(row_pos + rows < frames, segment(row_pos + rows), -2)
    prev_col = segment(col_pos - rows)
    bias_own[...] = jnp.where((own_col == own_row) & (col_pos <= row_pos), 0.0, MASKED)
    bias_prev[...] = jnp.where(prev_col == own_row, 0.0, MASKED)
    bias_next[...] = jnp.where(own_col == next_row, 0.0, MASKED)

    loads[0].wait()
    tail.wait()

    def tap_rows(tap):
        frame = lax.broadcasted_iota(jnp.int32, (1, rows), 1)
        feature = 2 * frame + (tap - 3)
        behind = 2 - lax.div(tap + 1, 2)
        live = segment(row_pos - behind) == own_row
        feature = jnp.where(live, feature, -1000)
        pick = lax.broadcasted_iota(jnp.int32, (2 * rows, rows), 0) == feature
        pick_tail = lax.broadcasted_iota(jnp.int32, (16, rows), 0) - 16 == feature
        picked = tn(hid[...], jnp.where(pick, 1.0, 0.0).astype(BF16))
        picked = picked + tn(tail_in[...], jnp.where(pick_tail, 1.0, 0.0).astype(BF16))
        return picked.astype(BF16)

    taps_copies = []
    for i in range(2):
        taps_out[i] = tap_rows(2 * (1 - core) + i)
        copy = remote(
            taps_out.at[i],
            taps_in.at[i],
            misc_send.at[2 + i],
            misc_recv.at[2 + i],
            {"dp": other_core},
        )
        copy.start()
        taps_copies.append(copy)
    for i in range(2):
        taps_mine[i] = tap_rows(2 * core + i)
    for load in loads[1:]:
        load.wait()

    def delta_of(g_head, o_head):
        product = g_head.astype(F32) * o_head.astype(F32)
        return jnp.sum(product.T, axis=0, keepdims=True)

    def scores(k_head, q_head, bias):
        return nt(k_head, q_head) * SCALE_LOG2E + bias[...]

    def grads(e, ratio, k_head, v_head, q_head, g_head, delta):
        prob = e * ratio
        d_value = nn(prob.astype(BF16), g_head)
        d_score = (prob * (nt(v_head, g_head) - delta)).astype(BF16)
        return d_value, nn(d_score, q_head) * SCALE, tn(k_head, d_score) * SCALE

    def stat_copies(index):
        return (
            remote(
                stat_own.at[index],
                stat_from_next.at[index],
                stat_send.at[index, 0],
                stat_recv.at[index, 0],
                {"ctx": before},
            ),
            remote(
                stat_next.at[index],
                stat_from_prev.at[index],
                stat_send.at[index, 1],
                stat_recv.at[index, 1],
                {"ctx": after},
            ),
        )

    def merged(m_one, z_one, m_two, z_two):
        m = jnp.maximum(m_one, m_two)
        z = z_one * jnp.exp2(m_one - m) + z_two * jnp.exp2(m_two - m)
        return jnp.exp2(m_one - m) / z

    def step(index, carry):
        here = cols(half_heads + index)
        for copy in qg_copies(index):
            copy.wait()
        s = scores(k[:, here], q[:, here], bias_own)
        m = jnp.max(s, axis=0, keepdims=True)
        e = jnp.exp2(s - m)
        e_own[...] = e
        stat_own[index, 0:1, :] = m
        stat_own[index, 1:2, :] = jnp.sum(e, axis=0, keepdims=True)
        stat_own[index, 2:3, :] = delta_of(g[:, here], o[:, here])
        s = scores(k[:, here], q_next[:, cols(index)], bias_next)
        m = jnp.max(s, axis=0, keepdims=True)
        e = jnp.exp2(s - m)
        e_next[...] = e
        stat_next[index, 0:1, :] = m
        stat_next[index, 1:2, :] = jnp.sum(e, axis=0, keepdims=True)
        for copy in stat_copies(index):
            copy.start()

        for copy in kv_copies(index):
            copy.wait()
        there = cols(index)
        s_own = scores(k[:, there], q[:, there], bias_own)
        s_prev = scores(k_prev[:, there], q[:, there], bias_prev)
        m = jnp.maximum(
            jnp.max(s_own, axis=0, keepdims=True), jnp.max(s_prev, axis=0, keepdims=True)
        )
        e_one = jnp.exp2(s_own - m)
        e_two = jnp.exp2(s_prev - m)
        ratio = 1.0 / (
            jnp.sum(e_one, axis=0, keepdims=True) + jnp.sum(e_two, axis=0, keepdims=True)
        )
        delta = delta_of(g[:, there], o[:, there])
        d_value, d_key, d_query = grads(
            e_one, ratio, k[:, there], v[:, there], q[:, there], g[:, there], delta
        )
        dv[:, there] = d_value.astype(BF16)
        dk[:, there] = d_key.astype(BF16)
        d_value, d_key, d_query_prev = grads(
            e_two, ratio, k_prev[:, there], v_prev[:, there], q[:, there], g[:, there], delta
        )
        dv_prev[:, there] = d_value.astype(BF16)
        dk_prev[:, there] = d_key.astype(BF16)
        dq[:, there] = (d_query + d_query_prev).T.astype(BF16)

        for copy in stat_copies(index):
            copy.wait()
        ratio = merged(
            stat_own[index, 0:1, :],
            stat_own[index, 1:2, :],
            stat_from_prev[index, 0:1, :],
            stat_from_prev[index, 1:2, :],
        )
        d_value, d_key, d_query = grads(
            e_own[...],
            ratio,
            k[:, here],
            v[:, here],
            q[:, here],
            g[:, here],
            stat_own[index, 2:3, :],
        )
        dq[:, here] = d_query.T.astype(BF16)
        ratio = merged(
            stat_next[index, 0:1, :],
            stat_next[index, 1:2, :],
            stat_from_next[index, 0:1, :],
            stat_from_next[index, 1:2, :],
        )
        d_value_next, d_key_next, d_query_next = grads(
            e_next[...],
            ratio,
            k[:, here],
            v[:, here],
            q_next[:, there],
            g_next[:, there],
            stat_from_next[index, 2:3, :],
        )
        dv[:, here] = (d_value + d_value_next).astype(BF16)
        dk[:, here] = (d_key + d_key_next).astype(BF16)
        dq_next[:, there] = d_query_next.T.astype(BF16)
        return carry

    lax.fori_loop(0, half_heads, step, 0)

    def piece(index):
        return pl.ds(pl.multiple_of(index * chunk, chunk), chunk)

    def back_copy(index):
        return remote(
            back_out.at[piece(index), :],
            back_in.at[piece(index), :],
            chunk_send.at[0, index],
            chunk_recv.at[0, index],
            {"ctx": before},
        )

    def fwd_copy(index):
        return remote(
            fwd_out.at[piece(index), :],
            fwd_in.at[piece(index), :],
            chunk_send.at[1, index],
            chunk_recv.at[1, index],
            {"ctx": after},
        )

    def pipe_copy(index):
        return remote(
            pipe_out.at[piece(index), :],
            pipe_in.at[piece(index), :],
            chunk_send.at[2, index],
            chunk_recv.at[2, index],
            {"pipe": 1 - pipe},
        )

    def half_copy(index):
        return remote(
            half_mine.at[piece(index), :],
            half_other.at[piece(index), :],
            chunk_send.at[3, index],
            chunk_recv.at[3, index],
            {"dp": other_core},
        )

    def project_away(index, carry):
        at = piece(index)
        fwd_out[at, :] = nt(dq_next[at, :], w[0, :, half_width:]).astype(BF16)
        fwd_copy(index).start()
        back = nt(dk_prev[at, :], w[1, :, :half_width]) + nt(dv_prev[at, :], w[2, :, :half_width])
        back_out[at, :] = back.astype(BF16)
        back_copy(index).start()
        return carry

    lax.fori_loop(0, CHUNKS, project_away, 0)

    def project_own(index, carry):
        at = piece(index)
        lat_sum[at, :] = nt(dq[at, :], w[0]) + nt(dk[at, :], w[1]) + nt(dv[at, :], w[2])
        return carry

    lax.fori_loop(0, CHUNKS, project_own, 0)

    def join_ctx(index, carry):
        at = piece(index)
        fwd_copy(index).wait()
        back_copy(index).wait()
        whole = lat_sum[at, :] + fwd_in[at, :].astype(F32) + back_in[at, :].astype(F32)
        lat_sum[at, :] = whole
        pipe_out[at, :] = whole.astype(BF16)
        pipe_copy(index).start()
        return carry

    lax.fori_loop(0, CHUNKS, join_ctx, 0)

    def join_pipe(index, carry):
        at = piece(index)
        pipe_copy(index).wait()
        latent = (lat_sum[at, :] + pipe_in[at, :].astype(F32)).astype(BF16)
        pipe_out[at, :] = latent
        ext[at, :] = latent.astype(F32)
        half_mine[at, :] = pipe_out[at, my_half]
        half_copy(index).start()
        return carry

    lax.fori_loop(0, CHUNKS, join_pipe, 0)
    lead = remote(
        pipe_out.at[pl.ds(0, 16), :], head_in, misc_send.at[4], misc_recv.at[4], {"ctx": before}
    )
    lead.start()

    for copy in taps_copies:
        copy.wait()

    def half_wait(index, carry):
        half_copy(index).wait()
        return carry

    lax.fori_loop(0, CHUNKS, half_wait, 0)
    for i in range(2):
        conv_part[i] = (
            nn(taps_mine[i], half_mine[...]) + nn(taps_in[i], half_other[...])
        ).astype(BF16)

    def rs_copy(step):
        to = lax.rem(ctx + step, n_ctx)
        return remote(
            conv_part.at[:, pl.ds(pl.multiple_of(to * share, share), share), :],
            conv_in.at[step],
            rs_send.at[step],
            rs_recv.at[step],
            {"ctx": to},
        )

    def rs_start(step, carry):
        rs_copy(step).start()
        return carry

    lax.fori_loop(1, n_ctx, rs_start, 0)

    lead.wait()
    swap.wait()
    ext[pl.ds(rows, 16), :] = head_in[...].astype(F32)

    def spread_tap(tap, shift):
        pos = col_pos + shift
        behind = (2, 1, 1, 0)[tap]
        live = (segment(pos - behind) == segment(pos)) & (pos < frames)
        masked = jnp.where(live, ext[pl.ds(shift, rows), :], 0.0).astype(BF16)
        return nt(masked, cw[tap])

    even = spread_tap(3, 0) + spread_tap(1, 1)
    odd = spread_tap(2, 1) + spread_tap(0, 2)
    for i in range(half // 128):
        at = slice(i * 128, (i + 1) * 128)
        spread[i, pl.ds(0, rows, stride=2), :] = even[:, at]
        spread[i, pl.ds(1, rows, stride=2), :] = odd[:, at]
        hid_out[:, at] = spread[i].astype(BF16)

    def rs_wait(step, carry):
        rs_copy(step).wait()
        return carry

    lax.fori_loop(1, n_ctx, rs_wait, 0)
    mine = conv_part[:, pl.ds(pl.multiple_of(ctx * share, share), share), :].astype(F32)
    total[dp] = lax.fori_loop(
        1, n_ctx, lambda step, carry: carry + conv_in[step].astype(F32), mine
    )

    copies = []
    for i in range(1, 4):
        copy = remote(
            total.at[dp], total.at[dp], dp_send.at[i], dp_recv.at[i], {"dp": lax.rem(dp + i, 4)}
        )
        copy.start()
        copies.append(copy)
    for i in range(1, 4):
        copies[i - 1].wait_send()
        sender = lax.rem(dp + 4 - i, 4)
        remote(
            total.at[sender], total.at[sender], dp_send.at[i], dp_recv.at[i], {"dp": sender}
        ).wait_recv()
    for side in range(2):
        conv_out[2 * side : 2 * side + 2] = total[side] + total[2 + side]


def body(queries, keys, values, outputs, out_grads, lengths, proj_weight, hidden, conv_weight):
    n_ctx = lax.axis_size("ctx")
    rows, width = queries.shape[1:]
    ch = proj_weight.shape[1]
    half = ch // 2
    half_width = width // 2
    half_heads = half_width // HEAD_DIM
    share = ch // n_ctx
    vmem = pltpu.VMEM
    dma = pltpu.SemaphoreType.DMA
    hidden_grad, conv_grad = pl.pallas_call(
        functools.partial(kernel, n_ctx),
        out_shape=(
            jax.ShapeDtypeStruct((2 * rows, half), BF16),
            jax.ShapeDtypeStruct((4, share, half), F32),
        ),
        in_specs=[pl.BlockSpec(memory_space=pltpu.SMEM)]
        + [pl.BlockSpec(memory_space=pl.ANY)] * 8,
        out_specs=(pl.BlockSpec(memory_space=pltpu.VMEM),) * 2,
        scratch_shapes=[vmem((rows, width), BF16)] * 5
        + [
            vmem((3, ch, width), BF16),
            vmem((2 * rows, ch), BF16),
            vmem((4, half, ch), BF16),
        ]
        + [vmem((rows, half_width), BF16)] * 4
        + [vmem((rows, rows), F32)] * 5
        + [vmem((half_heads, 8, rows), F32)] * 4
        + [vmem((rows, width), BF16)] * 3
        + [vmem((rows, half_width), BF16)] * 3
        + [vmem((rows, ch), F32)]
        + [vmem((rows, ch), BF16)] * 6
        + [vmem((rows, half), BF16)] * 2
        + [
            vmem((rows + 16, ch), F32),
            vmem((16, ch), BF16),
            vmem((16, ch), BF16),
        ]
        + [vmem((2, ch, rows), BF16)] * 3
        + [
            vmem((half // 128, 2 * rows, 128), F32),
            vmem((2, ch, half), BF16),
            vmem((n_ctx, 2, share, half), BF16),
            vmem((4, 2, share, half), F32),
            dma((8,)),
        ]
        + [dma((half_heads, 2))] * 6
        + [dma((4, CHUNKS))] * 2
        + [dma((5,))] * 2
        + [dma((n_ctx,))] * 2
        + [dma((4,))] * 2,
        compiler_params=pltpu.CompilerParams(
            collective_id=0, has_side_effects=True, vmem_limit_bytes=56 * 1024 * 1024
        ),
    )(
        lengths[0],
        queries[0],
        keys[0],
        values[0],
        outputs[0],
        out_grads[0],
        proj_weight,
        hidden[0],
        conv_weight,
    )
    return hidden_grad[None], conv_grad


def solution(mesh):
    placed = (
        P("dp", "ctx", "pipe"),
        P("dp", "ctx", "pipe"),
        P("dp", "ctx", "pipe"),
        P("dp", "ctx", "pipe"),
        P("dp", "ctx", "pipe"),
        P("dp", None),
        P(None, None, "pipe"),
        P("dp", "ctx", None),
        P(None, None, "pipe"),
    )
    return jax.shard_map(
        body,
        mesh=mesh,
        in_specs=placed,
        out_specs=(P("dp", "ctx", "pipe"), P(None, "ctx", "pipe")),
        check_vma=False,
    )
```

time: 1320 us -> 101 us (0.08)
  waiting for transfers between devices: 1220 us -> 0 us
  Pallas kernels: 0 us -> 96.9 us
  matrix products: 30.1 us -> 0 us
  starting transfers between devices: 16.8 us -> 0 us
  local copies, waits for them, and re-layouts: 18.1 us -> 3.34 us
  other arithmetic: 14.1 us -> 0 us
  between operations: 14.2 us -> 0.64 us
    psum x1 -> x0, waiting for transfers between devices: 1070 us -> none  [body(): total = lax.psum(local_taps, ('ctx', 'dp'))]
    pallas_call x0 -> x1, Pallas kernels: none -> 96.9 us  [body(): pl.pallas_call(functools.partial(kernel, n_ctx), out_shape=(jax.ShapeDtyp...]
    ppermute x6 -> x0, waiting for transfers between devices: 81.3 us -> none  [from_behind(): return lax.ppermute(shard, axis, pairs)]
    reduce_scatter x2 -> x0, waiting for transfers between devices: 65.2 us -> none  [the longest x1 37.6 us: body(): lax.psum_scatter(hidden_part, 'pipe', scatter_dimension=1, tiled=True)]
    dot_general x21 -> x0, matrix products: 30.1 us -> none  [the longest x2 7.18 us: pair_grads(): jnp.einsum('qhd,khd->hqk', grad_heads, value_heads, preferred_element_typ...]
    ppermute x6 -> x0, starting transfers between devices: 16.6 us -> none  [from_behind(): return lax.ppermute(shard, axis, pairs)]
  transfers between devices with their start and end apart: 9 -> 0, of which waited for: 7 -> 0; matrix products, arithmetic and copies ran while one was open for 4% -> 0% of each run, Pallas kernels for 0% -> 0%
where the time goes in v1:
time: 101 us
  Pallas kernels  96.9 us (96%)
  local copies, waits for them, and re-layouts  3.34 us (3%)
    pallas_call x1, Pallas kernels, body(): pl.pallas_call(functools.partial(kernel, n_ctx), out_shape=(jax.ShapeDtyp...  96.9 us
    unnamed x2, local copies, waits for them, and re-layouts  3.34 us

profile of v1, /device:TPU:1, one launch (start us, length us, event | category | flops | bytes accessed | tf_op | source)
XLA Modules:
  0.0 100.8 jit_solution(14238822610015450851)
XLA Ops:
  0.6 96.9 %shard_map.104 = (bf16[1024,256]{1,0:T(8,128)(2,1)}, f32[4,16,256]{2,1,0:T(8,128)}) custom-call(s32[4]{0:T(128)} %bitcast.15, bf16[512,1024]{1,0:T(8,128)(2,1)} %bitcast.8, bf16[512,1024]{1,0:T(8,128)(2,1)} %bitcast.9, bf16[512,1024]{1,0:T(8,128)(2,1)} %bitcast.10, bf16[512,1024]{1,0:T(8,128)(2,1)} %bitcast.11, bf16[512,1024]{1,0:T(8,128)(2,1)} %bitcast.12, ...), custom_call_target="tpu_custom_call" | custom-call | tf_op jit(solution)/shard_map/pallas_call | solution.py:577
  97.5 1.9 %copy.13 = bf16[1,1024,256]{2,1,0:T(8,128)(2,1)} copy(bf16[1,1024,256]{2,1,0:T(8,128)(2,1)} %bitcast.14) | data formatting | bytes 1048576
  99.4 1.5 %copy.14 = f32[4,16,256]{2,1,0:T(8,128)} copy(f32[4,16,256]{2,1,0:T(8,128)} %get-tuple-element.9) | data formatting | bytes 131072

commit v2 on v1

--- a/solution.py
+++ b/solution.py
@@ -10,7 +10,6 @@
 SCALE = HEAD_DIM ** (-0.5)
 SCALE_LOG2E = SCALE * 1.4426950408889634
 MASKED = -1e30
-CHUNKS = 4
 MESH = pl.DeviceIdType.MESH
 F32 = jnp.float32
 BF16 = jnp.bfloat16
@@ -47,6 +46,7 @@
     o,
     g,
     w,
+    wt,
     hid,
     cw,
     k_prev,
@@ -57,7 +57,6 @@
     bias_prev,
     bias_next,
     e_own,
-    e_next,
     stat_own,
     stat_next,
     stat_from_next,
@@ -68,11 +67,15 @@
     dk_prev,
     dv_prev,
     dq_next,
+    dq_part,
+    dk_part,
+    dv_part,
     lat_sum,
     back_out,
     back_in,
     fwd_out,
     fwd_in,
+    lat,
     pipe_out,
     pipe_in,
     half_mine,
@@ -94,8 +97,10 @@
     qg_recv,
     stat_send,
     stat_recv,
-    chunk_send,
-    chunk_recv,
+    z_send,
+    z_recv,
+    x_send,
+    x_recv,
     misc_send,
     misc_recv,
     rs_send,
@@ -111,7 +116,7 @@
     half = ch // 2
     frames = rows * n_ctx
     share = ch // n_ctx
-    chunk = rows // CHUNKS
+    chunk = rows // 2
     pipe = lax.axis_index("pipe")
     ctx = lax.axis_index("ctx")
     dp = lax.axis_index("dp")
@@ -140,11 +145,11 @@
         pltpu.make_async_copy(src, dst, local_sem.at[i])
         for i, (src, dst) in enumerate(
             (
-                (hid_in, hid),
                 (k_in, k),
                 (q_in, q),
                 (g_in, g),
                 (o_in, o),
+                (hid_in, hid),
                 (v_in, v),
                 (w_in, w),
                 (cw_in.at[:, my_half, :], cw.at[:, :, my_half]),
@@ -168,7 +173,55 @@
         pl.semaphore_signal(
             barrier, inc=1, device_id={"dp": lax.rem(dp + step, 4)}, device_id_type=MESH
         )
-    pl.semaphore_wait(barrier, n_ctx - 1 + 1 + 3)
+    for near in (after, before):
+        pl.semaphore_signal(
+            barrier, inc=1, device_id={"ctx": near, "pipe": 1 - pipe}, device_id_type=MESH
+        )
+
+    ends = [lengths[0]]
+    for i in range(1, 4):
+        ends.append(ends[-1] + lengths[i])
+
+    def segment(pos):
+        count = jnp.zeros(pos.shape, jnp.int32)
+        for end in ends:
+            count = count + jnp.where(pos >= end, 1, 0)
+        return jnp.where(pos >= 0, count, -1)
+
+    row_pos = start + lax.broadcasted_iota(jnp.int32, (1, rows), 1)
+    col_pos = start + lax.broadcasted_iota(jnp.int32, (rows, 1), 0)
+    own_row = segment(row_pos)
+    own_col = segment(col_pos)
+    next_row = jnp.where(row_pos + rows < frames, segment(row_pos + rows), -2)
+    prev_col = segment(col_pos - rows)
+    bias_own[...] = jnp.where((own_col == own_row) & (col_pos <= row_pos), 0.0, MASKED)
+    bias_prev[...] = jnp.where(prev_col == own_row, 0.0, MASKED)
+    bias_next[...] = jnp.where(own_col == next_row, 0.0, MASKED)
+
+    def delta_of(g_head, o_head):
+        product = g_head.astype(F32) * o_head.astype(F32)
+        return jnp.sum(product.T, axis=0, keepdims=True)
+
+    def statistics(k_head, q_head, bias):
+        s = nt(k_head, q_head) * SCALE_LOG2E + bias[...]
+        m = jnp.max(s, axis=0, keepdims=True)
+        e = jnp.exp2(s - m)
+        return e, m, jnp.sum(e, axis=0, keepdims=True)
+
+    for load in loads[:4]:
+        load.wait()
+
+    def own_statistics(index, carry):
+        here = cols(index)
+        e, m, z = statistics(k[:, here], q[:, here], bias_own)
+        e_own[index] = e
+        stat_own[index, 0:1, :] = m
+        stat_own[index, 1:2, :] = z
+        stat_own[index, 2:3, :] = delta_of(g[:, here], o[:, here])
+        return carry
+
+    lax.fori_loop(0, heads, own_statistics, 0)
+    pl.semaphore_wait(barrier, n_ctx - 1 + 1 + 3 + 2)
 
     tail = remote(
         hid_in.at[pl.ds(2 * rows - 16, 16), :],
@@ -178,6 +231,14 @@
         {"ctx": after},
     )
     tail.start()
+    totals = remote(
+        stat_own.at[pl.ds(half_heads, half_heads)],
+        stat_from_next,
+        misc_send.at[5],
+        misc_recv.at[5],
+        {"ctx": before},
+    )
+    totals.start()
 
     def kv_copies(index):
         return (
@@ -220,7 +281,7 @@
             copy.start()
         return carry
 
-    lax.fori_loop(0, half_heads, halo, 0)
+    lax.fori_loop(0, 2, halo, 0)
     swap = remote(
         cw_in.at[:, their_half, :],
         cw.at[:, :, my_half],
@@ -230,27 +291,8 @@
     )
     swap.start()
 
-    ends = [lengths[0]]
-    for i in range(1, 4):
-        ends.append(ends[-1] + lengths[i])
-
-    def segment(pos):
-        count = jnp.zeros(pos.shape, jnp.int32)
-        for end in ends:
-            count = count + jnp.where(pos >= end, 1, 0)
-        return jnp.where(pos >= 0, count, -1)
-
-    row_pos = start + lax.broadcasted_iota(jnp.int32, (1, rows), 1)
-    col_pos = start + lax.broadcasted_iota(jnp.int32, (rows, 1), 0)
-    own_row = segment(row_pos)
-    own_col = segment(col_pos)
-    next_row = jnp.where(row_pos + rows < frames, segment(row_pos + rows), -2)
-    prev_col = segment(col_pos - rows)
-    bias_own[...] = jnp.where((own_col == own_row) & (col_pos <= row_pos), 0.0, MASKED)
-    bias_prev[...] = jnp.where(prev_col == own_row, 0.0, MASKED)
-    bias_next[...] = jnp.where(own_col == next_row, 0.0, MASKED)
-
-    loads[0].wait()
+    for load in loads[4:]:
+        load.wait()
     tail.wait()
 
     def tap_rows(tap):
@@ -279,15 +321,9 @@
         taps_copies.append(copy)
     for i in range(2):
         taps_mine[i] = tap_rows(2 * core + i)
-    for load in loads[1:]:
-        load.wait()
-
-    def delta_of(g_head, o_head):
-        product = g_head.astype(F32) * o_head.astype(F32)
-        return jnp.sum(product.T, axis=0, keepdims=True)
-
-    def scores(k_head, q_head, bias):
-        return nt(k_head, q_head) * SCALE_LOG2E + bias[...]
+    for i in range(3):
+        wt[i] = w[i].T
+    totals.wait()
 
     def grads(e, ratio, k_head, v_head, q_head, g_head, delta):
         prob = e * ratio
@@ -295,85 +331,76 @@
         d_score = (prob * (nt(v_head, g_head) - delta)).astype(BF16)
         return d_value, nn(d_score, q_head) * SCALE, tn(k_head, d_score) * SCALE
 
-    def stat_copies(index):
-        return (
-            remote(
-                stat_own.at[index],
-                stat_from_next.at[index],
-                stat_send.at[index, 0],
-                stat_recv.at[index, 0],
-                {"ctx": before},
-            ),
-            remote(
-                stat_next.at[index],
-                stat_from_prev.at[index],
-                stat_send.at[index, 1],
-                stat_recv.at[index, 1],
-                {"ctx": after},
-            ),
+    def stat_copy(index):
+        return remote(
+            stat_next.at[index],
+            stat_from_prev.at[index],
+            stat_send.at[index],
+            stat_recv.at[index],
+            {"ctx": after},
         )
 
     def merged(m_one, z_one, m_two, z_two):
         m = jnp.maximum(m_one, m_two)
-        z = z_one * jnp.exp2(m_one - m) + z_two * jnp.exp2(m_two - m)
-        return jnp.exp2(m_one - m) / z
-
-    def step(index, carry):
+        weight = jnp.exp2(m_one - m)
+        other = jnp.exp2(m_two - m)
+        whole = z_one * weight + z_two * other
+        return weight / whole, other / whole
+
+    def cross_second(index):
         here = cols(half_heads + index)
+        there = cols(index)
         for copy in qg_copies(index):
             copy.wait()
-        s = scores(k[:, here], q[:, here], bias_own)
-        m = jnp.max(s, axis=0, keepdims=True)
-        e = jnp.exp2(s - m)
-        e_own[...] = e
-        stat_own[index, 0:1, :] = m
-        stat_own[index, 1:2, :] = jnp.sum(e, axis=0, keepdims=True)
-        stat_own[index, 2:3, :] = delta_of(g[:, here], o[:, here])
-        s = scores(k[:, here], q_next[:, cols(index)], bias_next)
-        m = jnp.max(s, axis=0, keepdims=True)
-        e = jnp.exp2(s - m)
-        e_next[...] = e
+        e, m, z = statistics(k[:, here], q_next[:, there], bias_next)
         stat_next[index, 0:1, :] = m
-        stat_next[index, 1:2, :] = jnp.sum(e, axis=0, keepdims=True)
-        for copy in stat_copies(index):
-            copy.start()
-
+        stat_next[index, 1:2, :] = z
+        stat_copy(index).start()
+
+        @pl.when(index + 2 < half_heads)
+        def _():
+            halo(index + 2, 0)
+
+        _, ratio = merged(
+            stat_from_next[index, 0:1, :], stat_from_next[index, 1:2, :], m, z
+        )
+        d_value, d_key, d_query = grads(
+            e,
+            ratio,
+            k[:, here],
+            v[:, here],
+            q_next[:, there],
+            g_next[:, there],
+            stat_from_next[index, 2:3, :],
+        )
+        dv_part[:, there] = d_value
+        dk_part[:, there] = d_key
+        dq_next[:, there] = d_query.T.astype(BF16)
+
+    def cross_first(index):
+        there = cols(index)
         for copy in kv_copies(index):
             copy.wait()
-        there = cols(index)
-        s_own = scores(k[:, there], q[:, there], bias_own)
-        s_prev = scores(k_prev[:, there], q[:, there], bias_prev)
-        m = jnp.maximum(
-            jnp.max(s_own, axis=0, keepdims=True), jnp.max(s_prev, axis=0, keepdims=True)
-        )
-        e_one = jnp.exp2(s_own - m)
-        e_two = jnp.exp2(s_prev - m)
-        ratio = 1.0 / (
-            jnp.sum(e_one, axis=0, keepdims=True) + jnp.sum(e_two, axis=0, keepdims=True)
-        )
-        delta = delta_of(g[:, there], o[:, there])
+        e, m, z = statistics(k_prev[:, there], q[:, there], bias_prev)
+        ratio_own, ratio = merged(stat_own[index, 0:1, :], stat_own[index, 1:2, :], m, z)
+        stat_own[index, 3:4, :] = ratio_own
         d_value, d_key, d_query = grads(
-            e_one, ratio, k[:, there], v[:, there], q[:, there], g[:, there], delta
-        )
-        dv[:, there] = d_value.astype(BF16)
-        dk[:, there] = d_key.astype(BF16)
-        d_value, d_key, d_query_prev = grads(
-            e_two, ratio, k_prev[:, there], v_prev[:, there], q[:, there], g[:, there], delta
+            e,
+            ratio,
+            k_prev[:, there],
+            v_prev[:, there],
+            q[:, there],
+            g[:, there],
+            stat_own[index, 2:3, :],
         )
         dv_prev[:, there] = d_value.astype(BF16)
         dk_prev[:, there] = d_key.astype(BF16)
-        dq[:, there] = (d_query + d_query_prev).T.astype(BF16)
-
-        for copy in stat_copies(index):
-            copy.wait()
-        ratio = merged(
-            stat_own[index, 0:1, :],
-            stat_own[index, 1:2, :],
-            stat_from_prev[index, 0:1, :],
-            stat_from_prev[index, 1:2, :],
-        )
-        d_value, d_key, d_query = grads(
-            e_own[...],
+        dq_part[index] = d_query
+
+    def own_grads(index, ratio):
+        here = cols(index)
+        return grads(
+            e_own[index],
             ratio,
             k[:, here],
             v[:, here],
@@ -381,113 +408,146 @@
             g[:, here],
             stat_own[index, 2:3, :],
         )
+
+    def own_first(index):
+        here = cols(index)
+        d_value, d_key, d_query = own_grads(index, stat_own[index, 3:4, :])
+        dv[:, here] = d_value.astype(BF16)
+        dk[:, here] = d_key.astype(BF16)
+        dq[:, here] = (d_query + dq_part[index]).T.astype(BF16)
+
+    def own_second(index):
+        here = cols(half_heads + index)
+        there = cols(index)
+        stat_copy(index).wait()
+        ratio, _ = merged(
+            stat_own[half_heads + index, 0:1, :],
+            stat_own[half_heads + index, 1:2, :],
+            stat_from_prev[index, 0:1, :],
+            stat_from_prev[index, 1:2, :],
+        )
+        d_value, d_key, d_query = own_grads(half_heads + index, ratio)
+        dv[:, here] = (d_value + dv_part[:, there]).astype(BF16)
+        dk[:, here] = (d_key + dk_part[:, there]).astype(BF16)
         dq[:, here] = d_query.T.astype(BF16)
-        ratio = merged(
-            stat_next[index, 0:1, :],
-            stat_next[index, 1:2, :],
-            stat_from_next[index, 0:1, :],
-            stat_from_next[index, 1:2, :],
-        )
-        d_value_next, d_key_next, d_query_next = grads(
-            e_next[...],
-            ratio,
-            k[:, here],
-            v[:, here],
-            q_next[:, there],
-            g_next[:, there],
-            stat_from_next[index, 2:3, :],
-        )
-        dv[:, here] = (d_value + d_value_next).astype(BF16)
-        dk[:, here] = (d_key + d_key_next).astype(BF16)
-        dq_next[:, there] = d_query_next.T.astype(BF16)
+
+    def step(index, carry):
+        pl.when(index >= 2)(lambda: own_second(index - 2))
+        cross_second(index)
+        cross_first(index)
+        pl.when(index < half_heads - 1)(lambda: own_first(index))
         return carry
 
     lax.fori_loop(0, half_heads, step, 0)
 
     def piece(index):
-        return pl.ds(pl.multiple_of(index * chunk, chunk), chunk)
+        side = lax.rem(index // 2 + 1 + pipe, 2)
+        at = pl.ds(pl.multiple_of(lax.rem(index, 2) * chunk, chunk), chunk)
+        return at, pl.ds(pl.multiple_of(side * half, half), half)
 
     def back_copy(index):
         return remote(
-            back_out.at[piece(index), :],
-            back_in.at[piece(index), :],
-            chunk_send.at[0, index],
-            chunk_recv.at[0, index],
+            back_out.at[piece(index)],
+            back_in.at[piece(index)],
+            z_send.at[0, index],
+            z_recv.at[0, index],
             {"ctx": before},
         )
 
     def fwd_copy(index):
         return remote(
-            fwd_out.at[piece(index), :],
-            fwd_in.at[piece(index), :],
-            chunk_send.at[1, index],
-            chunk_recv.at[1, index],
+            fwd_out.at[piece(index)],
+            fwd_in.at[piece(index)],
+            z_send.at[1, index],
+            z_recv.at[1, index],
             {"ctx": after},
         )
 
+    def x_copy(kind, src, dst, index, where):
+        at = pl.ds(pl.multiple_of(index * chunk, chunk), chunk)
+        return remote(
+            src.at[at], dst.at[at], x_send.at[kind, index], x_recv.at[kind, index], where
+        )
+
     def pipe_copy(index):
+        return x_copy(0, pipe_out, pipe_in, index, {"pipe": 1 - pipe})
+
+    def half_copy(index):
+        return x_copy(1, half_mine, half_other, index, {"dp": other_core})
+
+    def lat_copy(index, side):
+        at = pl.ds(pl.multiple_of(index * chunk, chunk), chunk)
         return remote(
-            pipe_out.at[piece(index), :],
-            pipe_in.at[piece(index), :],
-            chunk_send.at[2, index],
-            chunk_recv.at[2, index],
+            lat.at[at, side],
+            lat.at[at, side],
+            x_send.at[2, index],
+            x_recv.at[2, index],
             {"pipe": 1 - pipe},
         )
 
-    def half_copy(index):
-        return remote(
-            half_mine.at[piece(index), :],
-            half_other.at[piece(index), :],
-            chunk_send.at[3, index],
-            chunk_recv.at[3, index],
-            {"dp": other_core},
-        )
-
     def project_away(index, carry):
-        at = piece(index)
-        fwd_out[at, :] = nt(dq_next[at, :], w[0, :, half_width:]).astype(BF16)
+        at, side = piece(index)
+        fwd_out[at, side] = nn(dq_next[at, :], wt[0, half_width:, side]).astype(BF16)
         fwd_copy(index).start()
-        back = nt(dk_prev[at, :], w[1, :, :half_width]) + nt(dv_prev[at, :], w[2, :, :half_width])
-        back_out[at, :] = back.astype(BF16)
+        back = nn(dk_prev[at, :], wt[1, :half_width, side])
+        back = back + nn(dv_prev[at, :], wt[2, :half_width, side])
+        back_out[at, side] = back.astype(BF16)
         back_copy(index).start()
         return carry
 
-    lax.fori_loop(0, CHUNKS, project_away, 0)
-
-    def project_own(index, carry):
-        at = piece(index)
-        lat_sum[at, :] = nt(dq[at, :], w[0]) + nt(dk[at, :], w[1]) + nt(dv[at, :], w[2])
-        return carry
-
-    lax.fori_loop(0, CHUNKS, project_own, 0)
+    lax.fori_loop(0, 4, project_away, 0)
+
+    own_first(half_heads - 1)
+
+    def own_late(index, carry):
+        own_second(index)
+        return carry
+
+    lax.fori_loop(max(half_heads - 2, 0), half_heads, own_late, 0)
 
     def join_ctx(index, carry):
-        at = piece(index)
+        at, side = piece(index)
+        own = nn(dq[at, :], wt[0, :, side]) + nn(dk[at, :], wt[1, :, side])
+        own = own + nn(dv[at, :], wt[2, :, side])
         fwd_copy(index).wait()
         back_copy(index).wait()
-        whole = lat_sum[at, :] + fwd_in[at, :].astype(F32) + back_in[at, :].astype(F32)
-        lat_sum[at, :] = whole
-        pipe_out[at, :] = whole.astype(BF16)
-        pipe_copy(index).start()
-        return carry
-
-    lax.fori_loop(0, CHUNKS, join_ctx, 0)
+        whole = own + fwd_in[at, side].astype(F32) + back_in[at, side].astype(F32)
+
+        @pl.when(index < 2)
+        def _():
+            pipe_out[at, :] = whole.astype(BF16)
+            pipe_copy(index).start()
+
+        @pl.when(index >= 2)
+        def _():
+            lat_sum[at, :] = whole
+
+        return carry
+
+    lax.fori_loop(0, 4, join_ctx, 0)
 
     def join_pipe(index, carry):
-        at = piece(index)
+        at = pl.ds(pl.multiple_of(index * chunk, chunk), chunk)
         pipe_copy(index).wait()
         latent = (lat_sum[at, :] + pipe_in[at, :].astype(F32)).astype(BF16)
-        pipe_out[at, :] = latent
-        ext[at, :] = latent.astype(F32)
-        half_mine[at, :] = pipe_out[at, my_half]
+        half_mine[at, :] = latent
         half_copy(index).start()
-        return carry
-
-    lax.fori_loop(0, CHUNKS, join_pipe, 0)
-    lead = remote(
-        pipe_out.at[pl.ds(0, 16), :], head_in, misc_send.at[4], misc_recv.at[4], {"ctx": before}
-    )
-    lead.start()
+        lat[at, my_half] = latent
+        lat_copy(index, my_half).start()
+        return carry
+
+    lax.fori_loop(0, 2, join_pipe, 0)
+    leads = []
+    for i in range(2):
+        lead = remote(
+            half_mine.at[pl.ds(0, 16), :],
+            head_in.at[:, my_half],
+            misc_send.at[4 + 2 * i],
+            misc_recv.at[4 + 2 * i],
+            {"ctx": before, "pipe": pipe + i - 2 * i * pipe},
+        )
+        lead.start()
+        leads.append(lead)
 
     for copy in taps_copies:
         copy.wait()
@@ -496,7 +556,7 @@
         half_copy(index).wait()
         return carry
 
-    lax.fori_loop(0, CHUNKS, half_wait, 0)
+    lax.fori_loop(0, 2, half_wait, 0)
     for i in range(2):
         conv_part[i] = (
             nn(taps_mine[i], half_mine[...]) + nn(taps_in[i], half_other[...])
@@ -518,8 +578,20 @@
 
     lax.fori_loop(1, n_ctx, rs_start, 0)
 
-    lead.wait()
+    for i in range(2):
+        leads[i].wait_send()
+        remote(
+            head_in.at[:, my_half if i == 0 else their_half],
+            head_in.at[:, my_half if i == 0 else their_half],
+            misc_send.at[4 + 2 * i],
+            misc_recv.at[4 + 2 * i],
+            {"ctx": before},
+        ).wait_recv()
+    for i in range(2):
+        lat_copy(i, my_half).wait_send()
+        lat_copy(i, their_half).wait_recv()
     swap.wait()
+    ext[pl.ds(0, rows), :] = lat[...].astype(F32)
     ext[pl.ds(rows, 16), :] = head_in[...].astype(F32)
 
     def spread_tap(tap, shift):
@@ -586,17 +658,22 @@
         scratch_shapes=[vmem((rows, width), BF16)] * 5
         + [
             vmem((3, ch, width), BF16),
+            vmem((3, width, ch), BF16),
             vmem((2 * rows, ch), BF16),
             vmem((4, half, ch), BF16),
         ]
         + [vmem((rows, half_width), BF16)] * 4
-        + [vmem((rows, rows), F32)] * 5
-        + [vmem((half_heads, 8, rows), F32)] * 4
+        + [vmem((rows, rows), F32)] * 3
+        + [vmem((2 * half_heads, rows, rows), F32)]
+        + [vmem((2 * half_heads, 8, rows), F32)]
+        + [vmem((half_heads, 8, rows), F32)] * 3
         + [vmem((rows, width), BF16)] * 3
         + [vmem((rows, half_width), BF16)] * 3
-        + [vmem((rows, ch), F32)]
-        + [vmem((rows, ch), BF16)] * 6
-        + [vmem((rows, half), BF16)] * 2
+        + [vmem((half_heads, HEAD_DIM, rows), F32)]
+        + [vmem((rows, half_width), F32)] * 2
+        + [vmem((rows, half), F32)]
+        + [vmem((rows, ch), BF16)] * 5
+        + [vmem((rows, half), BF16)] * 4
         + [
             vmem((rows + 16, ch), F32),
             vmem((16, ch), BF16),
@@ -610,9 +687,11 @@
             vmem((4, 2, share, half), F32),
             dma((8,)),
         ]
-        + [dma((half_heads, 2))] * 6
-        + [dma((4, CHUNKS))] * 2
-        + [dma((5,))] * 2
+        + [dma((half_heads, 2))] * 4
+        + [dma((half_heads,))] * 2
+        + [dma((2, 4))] * 2
+        + [dma((3, 2))] * 2
+        + [dma((7,))] * 2
         + [dma((n_ctx,))] * 2
         + [dma((4,))] * 2,
         compiler_params=pltpu.CompilerParams(

time: 101 us -> 82.3 us (0.81)
  Pallas kernels: 96.9 us -> 78.2 us
    pallas_call x1, Pallas kernels: 96.9 us -> 78.2 us  [body(): pl.pallas_call(functools.partial(kernel, n_ctx), out_shape=(jax.ShapeDtyp...]
where the time goes in v2:
time: 82.3 us; the launch traced here: 82.2 us
  Pallas kernels  78.2 us (95%)
  local copies, waits for them, and re-layouts  3.34 us (4%)
    pallas_call x1, Pallas kernels, body(): pl.pallas_call(functools.partial(kernel, n_ctx), out_shape=(jax.ShapeDtyp...  78.2 us
    unnamed x2, local copies, waits for them, and re-layouts  3.34 us

profile of v2, /device:TPU:1, one launch (start us, length us, event | category | flops | bytes accessed | tf_op | source)
XLA Modules:
  0.0 82.2 jit_solution(3857065461917578432)
XLA Ops:
  0.6 78.2 %shard_map.104 = (bf16[1024,256]{1,0:T(8,128)(2,1)}, f32[4,16,256]{2,1,0:T(8,128)}) custom-call(s32[4]{0:T(128)} %bitcast.15, bf16[512,1024]{1,0:T(8,128)(2,1)} %bitcast.8, bf16[512,1024]{1,0:T(8,128)(2,1)} %bitcast.9, bf16[512,1024]{1,0:T(8,128)(2,1)} %bitcast.10, bf16[512,1024]{1,0:T(8,128)(2,1)} %bitcast.11, bf16[512,1024]{1,0:T(8,128)(2,1)} %bitcast.12, ...), custom_call_target="tpu_custom_call" | custom-call | tf_op jit(solution)/shard_map/pallas_call | solution.py:649
  78.8 1.9 %copy.13 = bf16[1,1024,256]{2,1,0:T(8,128)(2,1)} copy(bf16[1,1024,256]{2,1,0:T(8,128)(2,1)} %bitcast.14) | data formatting | bytes 1048576
  80.7 1.5 %copy.14 = f32[4,16,256]{2,1,0:T(8,128)} copy(f32[4,16,256]{2,1,0:T(8,128)} %get-tuple-element.9) | data formatting | bytes 131072

commit v3 on v2

--- a/solution.py
+++ b/solution.py
@@ -70,7 +70,6 @@
     dq_part,
     dk_part,
     dv_part,
-    lat_sum,
     back_out,
     back_in,
     fwd_out,
@@ -105,6 +104,8 @@
     misc_recv,
     rs_send,
     rs_recv,
+    lead_send,
+    lead_recv,
     dp_send,
     dp_recv,
 ):
@@ -116,7 +117,7 @@
     half = ch // 2
     frames = rows * n_ctx
     share = ch // n_ctx
-    chunk = rows // 2
+    quarter = half // 2
     pipe = lax.axis_index("pipe")
     ctx = lax.axis_index("ctx")
     dp = lax.axis_index("dp")
@@ -178,26 +179,6 @@
             barrier, inc=1, device_id={"ctx": near, "pipe": 1 - pipe}, device_id_type=MESH
         )
 
-    ends = [lengths[0]]
-    for i in range(1, 4):
-        ends.append(ends[-1] + lengths[i])
-
-    def segment(pos):
-        count = jnp.zeros(pos.shape, jnp.int32)
-        for end in ends:
-            count = count + jnp.where(pos >= end, 1, 0)
-        return jnp.where(pos >= 0, count, -1)
-
-    row_pos = start + lax.broadcasted_iota(jnp.int32, (1, rows), 1)
-    col_pos = start + lax.broadcasted_iota(jnp.int32, (rows, 1), 0)
-    own_row = segment(row_pos)
-    own_col = segment(col_pos)
-    next_row = jnp.where(row_pos + rows < frames, segment(row_pos + rows), -2)
-    prev_col = segment(col_pos - rows)
-    bias_own[...] = jnp.where((own_col == own_row) & (col_pos <= row_pos), 0.0, MASKED)
-    bias_prev[...] = jnp.where(prev_col == own_row, 0.0, MASKED)
-    bias_next[...] = jnp.where(own_col == next_row, 0.0, MASKED)
-
     def delta_of(g_head, o_head):
         product = g_head.astype(F32) * o_head.astype(F32)
         return jnp.sum(product.T, axis=0, keepdims=True)
@@ -208,19 +189,6 @@
         e = jnp.exp2(s - m)
         return e, m, jnp.sum(e, axis=0, keepdims=True)
 
-    for load in loads[:4]:
-        load.wait()
-
-    def own_statistics(index, carry):
-        here = cols(index)
-        e, m, z = statistics(k[:, here], q[:, here], bias_own)
-        e_own[index] = e
-        stat_own[index, 0:1, :] = m
-        stat_own[index, 1:2, :] = z
-        stat_own[index, 2:3, :] = delta_of(g[:, here], o[:, here])
-        return carry
-
-    lax.fori_loop(0, heads, own_statistics, 0)
     pl.semaphore_wait(barrier, n_ctx - 1 + 1 + 3 + 2)
 
     tail = remote(
@@ -231,15 +199,6 @@
         {"ctx": after},
     )
     tail.start()
-    totals = remote(
-        stat_own.at[pl.ds(half_heads, half_heads)],
-        stat_from_next,
-        misc_send.at[5],
-        misc_recv.at[5],
-        {"ctx": before},
-    )
-    totals.start()
-
     def kv_copies(index):
         return (
             remote(
@@ -281,7 +240,7 @@
             copy.start()
         return carry
 
-    lax.fori_loop(0, 2, halo, 0)
+    halo(0, 0)
     swap = remote(
         cw_in.at[:, their_half, :],
         cw.at[:, :, my_half],
@@ -291,9 +250,54 @@
     )
     swap.start()
 
+    ends = [lengths[0]]
+    for i in range(1, 4):
+        ends.append(ends[-1] + lengths[i])
+
+    def segment(pos):
+        count = jnp.zeros(pos.shape, jnp.int32)
+        for end in ends:
+            count = count + jnp.where(pos >= end, 1, 0)
+        return jnp.where(pos >= 0, count, -1)
+
+    row_pos = start + lax.broadcasted_iota(jnp.int32, (1, rows), 1)
+    col_pos = start + lax.broadcasted_iota(jnp.int32, (rows, 1), 0)
+    own_row = segment(row_pos)
+    own_col = segment(col_pos)
+    next_row = jnp.where(row_pos + rows < frames, segment(row_pos + rows), -2)
+    prev_col = segment(col_pos - rows)
+    bias_own[...] = jnp.where((own_col == own_row) & (col_pos <= row_pos), 0.0, MASKED)
+    bias_prev[...] = jnp.where(prev_col == own_row, 0.0, MASKED)
+    bias_next[...] = jnp.where(own_col == next_row, 0.0, MASKED)
+
+    for load in loads[:4]:
+        load.wait()
+
+    def own_statistics(index, carry):
+        here = cols(index)
+        e, m, z = statistics(k[:, here], q[:, here], bias_own)
+        e_own[index] = e
+        stat_own[index, 0:1, :] = m
+        stat_own[index, 1:2, :] = z
+        stat_own[index, 2:3, :] = delta_of(g[:, here], o[:, here])
+        return carry
+
+    lax.fori_loop(half_heads, heads, own_statistics, 0)
+    totals = remote(
+        stat_own.at[pl.ds(half_heads, half_heads)],
+        stat_from_next,
+        misc_send.at[5],
+        misc_recv.at[5],
+        {"ctx": before},
+    )
+    totals.start()
+    halo(1, 0)
+    lax.fori_loop(0, half_heads, own_statistics, 0)
     for load in loads[4:]:
         load.wait()
-    tail.wait()
+    for i in range(3):
+        wt[i] = w[i].T
+    totals.wait()
 
     def tap_rows(tap):
         frame = lax.broadcasted_iota(jnp.int32, (1, rows), 1)
@@ -307,6 +311,7 @@
         picked = picked + tn(tail_in[...], jnp.where(pick_tail, 1.0, 0.0).astype(BF16))
         return picked.astype(BF16)
 
+    tail.wait()
     taps_copies = []
     for i in range(2):
         taps_out[i] = tap_rows(2 * (1 - core) + i)
@@ -319,11 +324,6 @@
         )
         copy.start()
         taps_copies.append(copy)
-    for i in range(2):
-        taps_mine[i] = tap_rows(2 * core + i)
-    for i in range(3):
-        wt[i] = w[i].T
-    totals.wait()
 
     def grads(e, ratio, k_head, v_head, q_head, g_head, delta):
         prob = e * ratio
@@ -440,58 +440,71 @@
 
     lax.fori_loop(0, half_heads, step, 0)
 
+    def columns(side, index):
+        return pl.ds(pl.multiple_of(side * half + index * quarter, quarter), quarter)
+
     def piece(index):
-        side = lax.rem(index // 2 + 1 + pipe, 2)
-        at = pl.ds(pl.multiple_of(lax.rem(index, 2) * chunk, chunk), chunk)
-        return at, pl.ds(pl.multiple_of(side * half, half), half)
+        return columns(lax.rem(lax.rem(index, 2) + 1 + pipe, 2), index // 2)
 
     def back_copy(index):
+        at = piece(index)
         return remote(
-            back_out.at[piece(index)],
-            back_in.at[piece(index)],
+            back_out.at[:, at],
+            back_in.at[:, at],
             z_send.at[0, index],
             z_recv.at[0, index],
             {"ctx": before},
         )
 
     def fwd_copy(index):
+        at = piece(index)
         return remote(
-            fwd_out.at[piece(index)],
-            fwd_in.at[piece(index)],
+            fwd_out.at[:, at],
+            fwd_in.at[:, at],
             z_send.at[1, index],
             z_recv.at[1, index],
             {"ctx": after},
         )
 
     def x_copy(kind, src, dst, index, where):
-        at = pl.ds(pl.multiple_of(index * chunk, chunk), chunk)
+        return remote(src, dst, x_send.at[kind, index], x_recv.at[kind, index], where)
+
+    def pipe_copy(index):
+        return x_copy(0, pipe_out.at[index], pipe_in.at[index], index, {"pipe": 1 - pipe})
+
+    def half_copy(index):
+        return x_copy(1, half_mine.at[index], half_other.at[index], index, {"dp": other_core})
+
+    def lat_copy(index, side):
+        at = columns(side, index)
+        return x_copy(2, lat.at[:, at], lat.at[:, at], index, {"pipe": 1 - pipe})
+
+    def lead_copy(index, turn, side):
         return remote(
-            src.at[at], dst.at[at], x_send.at[kind, index], x_recv.at[kind, index], where
-        )
-
-    def pipe_copy(index):
-        return x_copy(0, pipe_out, pipe_in, index, {"pipe": 1 - pipe})
-
-    def half_copy(index):
-        return x_copy(1, half_mine, half_other, index, {"dp": other_core})
-
-    def lat_copy(index, side):
-        at = pl.ds(pl.multiple_of(index * chunk, chunk), chunk)
+            half_mine.at[index, pl.ds(0, 16), :],
+            head_in.at[:, columns(side, index)],
+            lead_send.at[index, turn],
+            lead_recv.at[index, turn],
+            {"ctx": before, "pipe": lax.rem(pipe + turn, 2)},
+        )
+
+    def rs_copy(index, step):
+        to = lax.rem(ctx + step, n_ctx)
         return remote(
-            lat.at[at, side],
-            lat.at[at, side],
-            x_send.at[2, index],
-            x_recv.at[2, index],
-            {"pipe": 1 - pipe},
+            conv_part.at[index, :, pl.ds(pl.multiple_of(to * share, share), share), :],
+            conv_in.at[index, step],
+            rs_send.at[index, step],
+            rs_recv.at[index, step],
+            {"ctx": to},
         )
 
     def project_away(index, carry):
-        at, side = piece(index)
-        fwd_out[at, side] = nn(dq_next[at, :], wt[0, half_width:, side]).astype(BF16)
+        at = piece(index)
+        fwd_out[:, at] = nn(dq_next[...], wt[0, half_width:, at]).astype(BF16)
         fwd_copy(index).start()
-        back = nn(dk_prev[at, :], wt[1, :half_width, side])
-        back = back + nn(dv_prev[at, :], wt[2, :half_width, side])
-        back_out[at, side] = back.astype(BF16)
+        back = nn(dk_prev[...], wt[1, :half_width, at])
+        back = back + nn(dv_prev[...], wt[2, :half_width, at])
+        back_out[:, at] = back.astype(BF16)
         back_copy(index).start()
         return carry
 
@@ -505,91 +518,64 @@
 
     lax.fori_loop(max(half_heads - 2, 0), half_heads, own_late, 0)
 
-    def join_ctx(index, carry):
-        at, side = piece(index)
-        own = nn(dq[at, :], wt[0, :, side]) + nn(dk[at, :], wt[1, :, side])
-        own = own + nn(dv[at, :], wt[2, :, side])
+    def project_own(index):
+        at = piece(index)
+        own = nn(dq[...], wt[0, :, at]) + nn(dk[...], wt[1, :, at])
+        return own + nn(dv[...], wt[2, :, at])
+
+    def join_ctx(index, own):
+        at = piece(index)
         fwd_copy(index).wait()
         back_copy(index).wait()
-        whole = own + fwd_in[at, side].astype(F32) + back_in[at, side].astype(F32)
-
-        @pl.when(index < 2)
-        def _():
-            pipe_out[at, :] = whole.astype(BF16)
-            pipe_copy(index).start()
-
-        @pl.when(index >= 2)
-        def _():
-            lat_sum[at, :] = whole
-
-        return carry
-
-    lax.fori_loop(0, 4, join_ctx, 0)
-
-    def join_pipe(index, carry):
-        at = pl.ds(pl.multiple_of(index * chunk, chunk), chunk)
+        return own + fwd_in[:, at].astype(F32) + back_in[:, at].astype(F32)
+
+    def give(index):
+        pipe_out[index] = join_ctx(2 * index, project_own(2 * index)).astype(BF16)
+        pipe_copy(index).start()
+
+    def settle(index, own):
+        whole = join_ctx(2 * index + 1, own)
         pipe_copy(index).wait()
-        latent = (lat_sum[at, :] + pipe_in[at, :].astype(F32)).astype(BF16)
-        half_mine[at, :] = latent
+        latent = (whole + pipe_in[index].astype(F32)).astype(BF16)
+        half_mine[index] = latent
         half_copy(index).start()
-        lat[at, my_half] = latent
-        lat_copy(index, my_half).start()
-        return carry
-
-    lax.fori_loop(0, 2, join_pipe, 0)
-    leads = []
+        lead_copy(index, 0, pipe).start()
+        lead_copy(index, 1, pipe).start()
+        lat[:, columns(pipe, index)] = latent
+        lat_copy(index, pipe).start()
+
+    def tap_grads(index):
+        half_copy(index).wait()
+        for i in range(2):
+            conv_part[index, i] = (
+                nn(taps_mine[i], half_mine[index]) + nn(taps_in[i], half_other[index])
+            ).astype(BF16)
+
+        def rs_start(step, carry):
+            rs_copy(index, step).start()
+            return carry
+
+        lax.fori_loop(1, n_ctx, rs_start, 0)
+
+    give(0)
     for i in range(2):
-        lead = remote(
-            half_mine.at[pl.ds(0, 16), :],
-            head_in.at[:, my_half],
-            misc_send.at[4 + 2 * i],
-            misc_recv.at[4 + 2 * i],
-            {"ctx": before, "pipe": pipe + i - 2 * i * pipe},
-        )
-        lead.start()
-        leads.append(lead)
-
+        taps_mine[i] = tap_rows(2 * core + i)
+    give(1)
+    own = project_own(1)
     for copy in taps_copies:
         copy.wait()
-
-    def half_wait(index, carry):
-        half_copy(index).wait()
-        return carry
-
-    lax.fori_loop(0, 2, half_wait, 0)
+    settle(0, own)
+    own = project_own(3)
+    tap_grads(0)
+    settle(1, own)
+    tap_grads(1)
+
     for i in range(2):
-        conv_part[i] = (
-            nn(taps_mine[i], half_mine[...]) + nn(taps_in[i], half_other[...])
-        ).astype(BF16)
-
-    def rs_copy(step):
-        to = lax.rem(ctx + step, n_ctx)
-        return remote(
-            conv_part.at[:, pl.ds(pl.multiple_of(to * share, share), share), :],
-            conv_in.at[step],
-            rs_send.at[step],
-            rs_recv.at[step],
-            {"ctx": to},
-        )
-
-    def rs_start(step, carry):
-        rs_copy(step).start()
-        return carry
-
-    lax.fori_loop(1, n_ctx, rs_start, 0)
-
-    for i in range(2):
-        leads[i].wait_send()
-        remote(
-            head_in.at[:, my_half if i == 0 else their_half],
-            head_in.at[:, my_half if i == 0 else their_half],
-            misc_send.at[4 + 2 * i],
-            misc_recv.at[4 + 2 * i],
-            {"ctx": before},
-        ).wait_recv()
-    for i in range(2):
-        lat_copy(i, my_half).wait_send()
-        lat_copy(i, their_half).wait_recv()
+        for turn in range(2):
+            lead_copy(i, turn, pipe).wait_send()
+            lead_copy(i, turn, lax.rem(pipe + turn, 2)).wait_recv()
+        lat_copy(i, pipe).wait_send()
+        lat_copy(i, 1 - pipe).wait_recv()
     swap.wait()
     ext[pl.ds(0, rows), :] = lat[...].astype(F32)
     ext[pl.ds(rows, 16), :] = head_in[...].astype(F32)
@@ -609,31 +595,39 @@
         spread[i, pl.ds(1, rows, stride=2), :] = odd[:, at]
         hid_out[:, at] = spread[i].astype(BF16)
 
-    def rs_wait(step, carry):
-        rs_copy(step).wait()
+    def dp_copy(index, turn, at):
+        return remote(
+            total.at[at, index],
+            total.at[at, index],
+            dp_send.at[index, turn],
+            dp_recv.at[index, turn],
+            {"dp": lax.rem(dp + turn, 4)},
+        )
+
+    def finish(index, carry):
+        def rs_add(step, carry):
+            rs_copy(index, step).wait()
+            return carry + conv_in[index, step].astype(F32)
+
+        mine = conv_part[index, :, pl.ds(pl.multiple_of(ctx * share, share), share), :]
+        total[dp, index] = lax.fori_loop(1, n_ctx, rs_add, mine.astype(F32))
+        for turn in range(1, 4):
+            dp_copy(index, turn, dp).start()
         return carry
 
-    lax.fori_loop(1, n_ctx, rs_wait, 0)
-    mine = conv_part[:, pl.ds(pl.multiple_of(ctx * share, share), share), :].astype(F32)
-    total[dp] = lax.fori_loop(
-        1, n_ctx, lambda step, carry: carry + conv_in[step].astype(F32), mine
-    )
-
-    copies = []
-    for i in range(1, 4):
-        copy = remote(
-            total.at[dp], total.at[dp], dp_send.at[i], dp_recv.at[i], {"dp": lax.rem(dp + i, 4)}
-        )
-        copy.start()
-        copies.append(copy)
-    for i in range(1, 4):
-        copies[i - 1].wait_send()
-        sender = lax.rem(dp + 4 - i, 4)
-        remote(
-            total.at[sender], total.at[sender], dp_send.at[i], dp_recv.at[i], {"dp": sender}
-        ).wait_recv()
-    for side in range(2):
-        conv_out[2 * side : 2 * side + 2] = total[side] + total[2 + side]
+    lax.fori_loop(0, 2, finish, 0)
+    for index in range(2):
+        for turn in range(1, 4):
+            dp_copy(index, turn, dp).wait_send()
+            dp_copy(index, turn, lax.rem(dp + 4 - turn, 4)).wait_recv()
+        at = slice(index * quarter, (index + 1) * quarter)
+        for side in range(2):
+            conv_out[2 * side : 2 * side + 2, :, at] = total[side, index] + total[2 + side, index]
+
+
+def hand_on(hid_in, conv_in, hid_out, conv_out):
+    hid_out[...] = hid_in[...]
+    conv_out[...] = conv_in[...]
 
 
 def body(queries, keys, values, outputs, out_grads, lengths, proj_weight, hidden, conv_weight):
@@ -671,9 +665,8 @@
         + [vmem((rows, half_width), BF16)] * 3
         + [vmem((half_heads, HEAD_DIM, rows), F32)]
         + [vmem((rows, half_width), F32)] * 2
-        + [vmem((rows, half), F32)]
         + [vmem((rows, ch), BF16)] * 5
-        + [vmem((rows, half), BF16)] * 4
+        + [vmem((2, rows, half // 2), BF16)] * 4
         + [
             vmem((rows + 16, ch), F32),
             vmem((16, ch), BF16),
@@ -682,18 +675,19 @@
         + [vmem((2, ch, rows), BF16)] * 3
         + [
             vmem((half // 128, 2 * rows, 128), F32),
-            vmem((2, ch, half), BF16),
-            vmem((n_ctx, 2, share, half), BF16),
-            vmem((4, 2, share, half), F32),
+            vmem((2, 2, ch, half // 2), BF16),
+            vmem((2, n_ctx, 2, share, half // 2), BF16),
+            vmem((4, 2, 2, share, half // 2), F32),
             dma((8,)),
         ]
         + [dma((half_heads, 2))] * 4
         + [dma((half_heads,))] * 2
         + [dma((2, 4))] * 2
         + [dma((3, 2))] * 2
-        + [dma((7,))] * 2
-        + [dma((n_ctx,))] * 2
-        + [dma((4,))] * 2,
+        + [dma((6,))] * 2
+        + [dma((2, n_ctx))] * 2
+        + [dma((2, 2))] * 2
+        + [dma((2, 4))] * 2,
         compiler_params=pltpu.CompilerParams(
             collective_id=0, has_side_effects=True, vmem_limit_bytes=56 * 1024 * 1024
         ),
@@ -708,6 +702,15 @@
         hidden[0],
         conv_weight,
     )
+    hidden_grad, conv_grad = pl.pallas_call(
+        hand_on,
+        out_shape=(
+            jax.ShapeDtypeStruct(hidden_grad.shape, BF16),
+            jax.ShapeDtypeStruct(conv_grad.shape, F32),
+        ),
+        in_specs=[pl.BlockSpec(memory_space=pltpu.VMEM)] * 2,
+        out_specs=(pl.BlockSpec(memory_space=pltpu.VMEM),) * 2,
+    )(hidden_grad, conv_grad)
     return hidden_grad[None], conv_grad
 
 

time: 82.3 us -> 78.2 us (0.950)
  local copies, waits for them, and re-layouts: 3.34 us -> 0 us
    unnamed x2 -> x0, local copies, waits for them, and re-layouts: 3.34 us -> none
    pallas_call x1, Pallas kernels: 78.2 us -> 75.5 us  [body(): pl.pallas_call(functools.partial(kernel, n_ctx), out_shape=(jax.ShapeDtyp...]
    pallas_call x0 -> x1, Pallas kernels: none -> 1.88 us  [body(): pl.pallas_call(hand_on, out_shape=(jax.ShapeDtypeStruct(hidden_grad.shape...]
where the time goes in v3:
time: 78.2 us; the launch traced here: 78.1 us
  Pallas kernels  77.4 us (99%)
    pallas_call x1, Pallas kernels, body(): pl.pallas_call(functools.partial(kernel, n_ctx), out_shape=(jax.ShapeDtyp...  75.5 us
    pallas_call x1, Pallas kernels, body(): pl.pallas_call(hand_on, out_shape=(jax.ShapeDtypeStruct(hidden_grad.shape...  1.88 us

profile of v3, /device:TPU:1, one launch (start us, length us, event | category | flops | bytes accessed | tf_op | source)
XLA Modules:
  0.0 78.1 jit_solution(14073819229184027090)
XLA Ops:
  0.6 75.5 %shard_map.104 = (bf16[1024,256]{1,0:T(8,128)(2,1)}, f32[4,16,256]{2,1,0:T(8,128)}) custom-call(s32[4]{0:T(128)} %bitcast.14, bf16[512,1024]{1,0:T(8,128)(2,1)} %bitcast.8, bf16[512,1024]{1,0:T(8,128)(2,1)} %bitcast.9, bf16[512,1024]{1,0:T(8,128)(2,1)} %bitcast.10, bf16[512,1024]{1,0:T(8,128)(2,1)} %bitcast.11, bf16[512,1024]{1,0:T(8,128)(2,1)} %bitcast.12, ...), custom_call_target="tpu_custom_call" | custom-call | tf_op jit(solution)/shard_map/pallas_call | solution.py:643
  76.2 1.9 %shard_map.105 = (bf16[1024,256]{1,0:T(8,128)(2,1)}, f32[4,16,256]{2,1,0:T(8,128)}) custom-call(bf16[1024,256]{1,0:T(8,128)(2,1)} %get-tuple-element.6.hid_in, f32[4,16,256]{2,1,0:T(8,128)} %get-tuple-element.7.conv_in), custom_call_target="tpu_custom_call" | custom-call | tf_op jit(solution)/shard_map/pallas_call | solution.py:705

commit v4 on v3

--- a/solution.py
+++ b/solution.py
@@ -605,12 +605,14 @@
         )
 
     def finish(index, carry):
-        def rs_add(step, carry):
+        def rs_wait(step, carry):
             rs_copy(index, step).wait()
-            return carry + conv_in[index, step].astype(F32)
-
+            return carry
+
+        lax.fori_loop(1, n_ctx, rs_wait, 0)
         mine = conv_part[index, :, pl.ds(pl.multiple_of(ctx * share, share), share), :]
-        total[dp, index] = lax.fori_loop(1, n_ctx, rs_add, mine.astype(F32))
+        arrived = jnp.sum(conv_in[index, 1:].astype(F32), axis=0)
+        total[dp, index] = mine.astype(F32) + arrived
         for turn in range(1, 4):
             dp_copy(index, turn, dp).start()
         return carry

time: 78.2 us -> 78.2 us (level)
  no operation moved by 1% of the time
where the time goes in v4:
time: 78.2 us; the launch traced here: 78.1 us
  Pallas kernels  77.4 us (99%)
    pallas_call x1, Pallas kernels, body(): pl.pallas_call(functools.partial(kernel, n_ctx), out_shape=(jax.ShapeDtyp...  75.6 us
    pallas_call x1, Pallas kernels, body(): pl.pallas_call(hand_on, out_shape=(jax.ShapeDtypeStruct(hidden_grad.shape...  1.88 us

profile of v4, /device:TPU:1, one launch (start us, length us, event | category | flops | bytes accessed | tf_op | source)
XLA Modules:
  0.0 78.1 jit_solution(8608784561551123767)
XLA Ops:
  0.6 75.6 %shard_map.104 = (bf16[1024,256]{1,0:T(8,128)(2,1)}, f32[4,16,256]{2,1,0:T(8,128)}) custom-call(s32[4]{0:T(128)} %bitcast.14, bf16[512,1024]{1,0:T(8,128)(2,1)} %bitcast.8, bf16[512,1024]{1,0:T(8,128)(2,1)} %bitcast.9, bf16[512,1024]{1,0:T(8,128)(2,1)} %bitcast.10, bf16[512,1024]{1,0:T(8,128)(2,1)} %bitcast.11, bf16[512,1024]{1,0:T(8,128)(2,1)} %bitcast.12, ...), custom_call_target="tpu_custom_call" | custom-call | tf_op jit(solution)/shard_map/pallas_call | solution.py:645
  76.2 1.9 %shard_map.105 = (bf16[1024,256]{1,0:T(8,128)(2,1)}, f32[4,16,256]{2,1,0:T(8,128)}) custom-call(bf16[1024,256]{1,0:T(8,128)(2,1)} %get-tuple-element.6.hid_in, f32[4,16,256]{2,1,0:T(8,128)} %get-tuple-element.7.conv_in), custom_call_target="tpu_custom_call" | custom-call | tf_op jit(solution)/shard_map/pallas_call | solution.py:707
